TPU v7x, 32 devices: a whole 2x2x4 slice. The times are simulated.
32 devices in a mesh: groups: 2 (over y), sub: 4 (over z), coarse: 2 (over x), rep: 2 (over core).
Axes of the slice: x: 2, y: 2, z: 4, core: 2. Of those that a mesh axis runs over, the one named last changes fastest.
Arguments:
- residual: float32 [8, 2, 19200], P('rep', None, ('groups', 'sub', 'coarse')), parts along dimension 2, may hold values from -24 to 24
- elem_inv: bfloat16 [16, 720000], P(('groups', 'sub', 'coarse')), parts along dimension 0, may hold values from -2 to 2.5
- elem_faces: int32 [256, 6], P(('groups', 'sub', 'coarse')), parts along dimension 0, may hold values from -1 to 79, as said below
- send_faces: int32 [16, 4, 8], P(('groups', 'sub', 'coarse')), parts along dimension 0, may hold values from -1 to 47, as said below
- coarse_basis: bfloat16 [2, 1024, 1200], P(None, ('groups', 'sub', 'coarse')), parts along dimension 1, may hold values from -0.29882812 to 0.29882812
- coarse_inv: bfloat16 [2, 1024, 512], P(None, ('groups', 'sub', 'coarse', 'rep')), parts along dimension 1, may hold values from -0.05 to 0.05, as said below
Outputs:
- precond: float32 [8, 2, 19200], P('rep', None, ('groups', 'sub', 'coarse')), parts along dimension 2
- inner: float32 [16, 2], P(('groups', 'rep')), parts along dimension 0
There are 2 independent parts, one for each index of `groups`. A program takes and returns all parts, laid end to end along the dimension named above; each array names one. Nothing has to cross between parts.
Inputs may be any that keep to these rules, and one draw needn't show every extreme that they name: `send_faces`: entries 0 or more are distinct within one subdomain. Slot j of subdomain s lists the faces read by subdomain s - o_j, o = (-2, -1, 1, 2), as many as that subdomain's halo slots with live entries; -1 marks an empty slot. For every subdomain s >= 2, slot 3 is full. `elem_faces`: values 48 + j * 8 + c name received faces; every live received face of a subdomain appears exactly once, every owned face once or twice; -1 is a boundary slot. Complex symmetric: coarse_inv[c, i, k] equals coarse_inv[c, k, i].
All inputs are finite; a program needn't handle non-finite values.
Results may differ from a plain program's by a relative error of at most 0.0003.
The roundings to bfloat16 on the way count: a program that leaves them out, or rounds other values in their place, can miss the bound.
Values may be sent and summed in bfloat16 or wider, within the bound.
A program may use at most 64 MiB of HBM per device.

v0:
```python
import jax
import jax.numpy as jnp
from jax import lax
from jax.sharding import PartitionSpec as P

FACE_DOF = 25


NEIGHBOUR_OFFSETS = (-2, -1, 1, 2)


def passed_along(array, axis, by):
    devices = lax.axis_size(axis)
    pairs = [(i, i + by) for i in range(devices) if 0 <= i + by < devices]
    return lax.ppermute(array, axis, pairs)


def contract_last(left, right):
    return lax.dot_general(
        left, right, (((1,), (1,)), ((), ())), preferred_element_type=jnp.float32
    )


def contract_first(left, right):
    return lax.dot_general(
        left, right, (((0,), (0,)), ((), ())), preferred_element_type=jnp.float32
    )


def apply_ops(ops, vec):
    return jnp.einsum("eij,sej->sei", ops, vec, preferred_element_type=jnp.float32)


def on_device(residual, elem_inv, elem_faces, send_faces, coarse_basis, coarse_inv):
    rounded = residual.astype(jnp.bfloat16)
    nsrc = residual.shape[0]
    length = residual.shape[2]
    owned = length // FACE_DOF
    capacity = send_faces.shape[2]
    nelem = elem_faces.shape[0]
    edof = 6 * FACE_DOF
    dead = owned + 4 * capacity
    faces = rounded.reshape(nsrc, 2, owned, FACE_DOF)
    zero_face = jnp.zeros((nsrc, 2, 1, FACE_DOF), jnp.bfloat16)
    padded = jnp.concatenate([faces, zero_face], 2)
    outgoing = jnp.where(send_faces[0] < 0, owned, send_faces[0])
    received = []
    for slot, offset in enumerate(NEIGHBOUR_OFFSETS):
        packed = padded[:, :, outgoing[slot]]
        received.append(passed_along(packed, ("sub", "coarse"), -offset))
    extended = jnp.concatenate([faces] + received + [zero_face], 2)
    lookup = jnp.where(elem_faces < 0, dead, elem_faces).reshape(-1)
    vectors = extended[:, :, lookup].reshape(nsrc, 2, nelem, edof)
    vec_re = vectors[:, 0]
    vec_im = vectors[:, 1]
    operators = elem_inv.reshape(nelem, 2, edof, edof)
    op_re = operators[:, 0]
    op_im = operators[:, 1]
    out_re = apply_ops(op_re, vec_re) - apply_ops(op_im, vec_im)
    out_im = apply_ops(op_re, vec_im) + apply_ops(op_im, vec_re)
    local = jnp.stack([out_re, out_im], 1).reshape(nsrc, 2, nelem * 6, FACE_DOF)
    summed = jax.ops.segment_sum(jnp.moveaxis(local, 2, 0), lookup, num_segments=dead + 1)
    returned = []
    for slot, offset in enumerate(NEIGHBOUR_OFFSETS):
        section = summed[owned + slot * capacity : owned + (slot + 1) * capacity]
        returned.append(passed_along(section, ("sub", "coarse"), offset))
    back_sum = jax.ops.segment_sum(
        jnp.concatenate(returned, 0), outgoing.reshape(-1), num_segments=owned + 1
    )
    fine = jnp.moveaxis(summed[:owned] + back_sum[:owned], 0, 2).reshape(nsrc, 2, length)
    basis_re = coarse_basis[0]
    basis_im = coarse_basis[1]
    res_re = rounded[:, 0]
    res_im = rounded[:, 1]
    real_real = contract_last(basis_re, res_re)
    imag_imag = contract_last(basis_im, res_im)
    real_imag = contract_last(basis_re, res_im)
    imag_real = contract_last(basis_im, res_re)
    restricted_b = jnp.stack([real_real - imag_imag, real_imag + imag_real]).astype(jnp.bfloat16)
    everyone = lax.all_gather(restricted_b, "rep", axis=2, tiled=True)
    piece = lax.all_gather(everyone, ("sub", "coarse"), axis=1, tiled=True)
    new_re = jnp.dot(coarse_inv[0], piece[0], preferred_element_type=jnp.float32) - jnp.dot(
        coarse_inv[1], piece[1], preferred_element_type=jnp.float32
    )
    new_im = jnp.dot(coarse_inv[0], piece[1], preferred_element_type=jnp.float32) + jnp.dot(
        coarse_inv[1], piece[0], preferred_element_type=jnp.float32
    )
    coeffs = jnp.stack([new_re, new_im])
    coeff_b = coeffs.astype(jnp.bfloat16)
    local_coeff = lax.all_to_all(coeff_b, "rep", split_axis=2, concat_axis=1, tiled=True)
    coarse_re = contract_first(local_coeff[0], basis_re) - contract_first(local_coeff[1], basis_im)
    coarse_im = contract_first(local_coeff[0], basis_im) + contract_first(local_coeff[1], basis_re)
    precond = fine + jnp.stack([coarse_re, coarse_im], 1)
    total = length * lax.axis_size(("sub", "coarse"))
    rounded_f = rounded.astype(jnp.float32)
    part_re = jnp.sum(rounded_f[:, 0] * precond[:, 0] + rounded_f[:, 1] * precond[:, 1], -1)
    part_im = jnp.sum(rounded_f[:, 0] * precond[:, 1] - rounded_f[:, 1] * precond[:, 0], -1)
    inner = lax.psum(jnp.stack([part_re, part_im], 1), ("sub", "coarse")) / total
    return (precond, inner)


def solution(mesh):
    placed = (
        P("rep", None, ("groups", "sub", "coarse")),
        P(("groups", "sub", "coarse"), None),
        P(("groups", "sub", "coarse"), None),
        P(("groups", "sub", "coarse"), None, None),
        P(None, ("groups", "sub", "coarse"), None),
        P(None, ("groups", "sub", "coarse", "rep"), None),
    )
    return jax.shard_map(
        on_device,
        mesh=mesh,
        in_specs=placed,
        out_specs=(P("rep", None, ("groups", "sub", "coarse")), P(("groups", "rep"), None)),
        check_vma=False,
    )
```

profile of v0, /device:TPU:0, one launch (start us, length us, event | category | flops | bytes accessed | tf_op | source)
XLA Modules:
  0.0 152.5 jit_solution(16921829606290808795)
XLA Ops:
  0.7 1.6 %fusion.55 = (f32[4,2,1200]{2,0,1:T(4,128)}, bf16[4,2,1200]{2,0,1:T(4,128)(2,1)S(1)}) fusion(f32[4,2,1200]{2,1,0:T(2,128)} %param.6), kind=kLoop, calls=%fused_computation.107 | loop fusion | flops 9600 | bytes 96000 | tf_op jit(solution)/shard_map/convert_element_type | solution.py:95
  3.8 1.2 gather_fusion
  5.0 5.5 %collective-permute-start = (bf16[4,2,8,25]{3,0,1,2:T(4,128)(2,1)}, bf16[4,2,8,25]{3,0,1,2:T(4,128)(2,1)}, u32[]{:S(2)}, u32[]{:S(2)}) collective-permute-start(bf16[4,2,8,25]{3,0,1,2:T(4,128)(2,1)} %bitcast.3), channel_id=1, source_target_pairs={{0,4},{2,6},{4,8},{6,10},{8,12},{10,14},{1,5},{3,7},{5,9},{7,11},{... | collective-permute-start | bytes 9608 | tf_op jit(solution)/shard_map/ppermute | solution.py:15
  10.5 1.2 gather_fusion.1
  11.7 4.0 %collective-permute-start.1 = (bf16[4,2,8,25]{3,0,1,2:T(4,128)(2,1)}, bf16[4,2,8,25]{3,0,1,2:T(4,128)(2,1)}, u32[]{:S(2)}, u32[]{:S(2)}) collective-permute-start(bf16[4,2,8,25]{3,0,1,2:T(4,128)(2,1)} %bitcast.6), channel_id=1, source_target_pairs={{0,2},{2,4},{4,6},{6,8},{8,10},{10,12},{12,14},{1,3},{3,5},{5,7},{... | collective-permute-start | bytes 9608 | tf_op jit(solution)/shard_map/ppermute | solution.py:15
  15.7 1.2 gather_fusion.2
  16.9 1.3 collective-permute-start.2
  18.2 1.2 gather_fusion.3
  19.3 1.3 collective-permute-start.3
  21.7 1.1 fusion.25
  22.7 1.1 fusion.10
  25.0 1.8 %all_gather.6 = bf16[2,64,8]{1,0,2:T(2,128)(2,1)S(1)} all-gather(bf16[2,64,4]{1,0,2:T(2,128)(2,1)S(1)} %copy.114), channel_id=1, replica_groups=mesh['groups'=2,'sub'=4,'coarse'=2,'rep'=2] {'rep'}, dimensions={2}, use_global_device_ids=true | all-gather | bytes 3072 | tf_op jit(solution)/shard_map/all_gather | solution.py:80
  26.8 33.8 %all_gather.7 = bf16[2,512,8]{2,0,1:T(2,128)(2,1)S(1)} all-gather(bf16[2,64,8]{2,0,1:T(2,128)(2,1)S(1)} %copy.115), channel_id=1, replica_groups=mesh['groups'=2,'sub'=4,'coarse'=2,'rep'=2] {'sub','coarse'}, dimensions={1}, use_global_device_ids=true | all-gather | bytes 18432 | tf_op jit(solution)/shard_map/all_gather | solution.py:81
  64.1 3.2 %all-to-all-start = ((bf16[2,2,128]{2,1,0:T(2,128)(2,1)}), bf16[2,2,128]{2,1,0:T(2,128)(2,1)S(1)}, u32[]{:S(2)}, u32[]{:S(2)}) async-start(bf16[2,2,128]{2,1,0:T(2,128)(2,1)} %reshape.255), calls=%async_computation | async-start | bytes 2048 | tf_op jit(solution)/shard_map/all_to_all | solution.py:90
  70.2 31.0 %reduce.2 = bf16[720000]{0:T(1024)(128)(2,1)} reduce(bf16[1,720000]{1,0:T(2,128)(2,1)S(1)} %copy-done, bf16[]{:T(256)} %constant.26), dimensions={0}, to_apply=%param.7.reduce_sub_computation | reduce | bytes 2880002 | tf_op args[1]
  101.2 5.2 %reshape.193 = bf16[16,2,150,150]{3,2,1,0:T(8,128)(2,1)S(1)} reshape(bf16[720000]{0:T(1024)(128)(2,1)} %reduce.2) | data formatting | bytes 2880000 | tf_op jit(solution)/shard_map/reshape | solution.py:56
  113.1 4.1 %scatter_fusion = f32[81,4,2,25]{3,1,2,0:T(4,128)S(1)} fusion(f32[81,4,2,25]{3,1,2,0:T(4,128)S(1)} %broadcast_in_dim.24, s32[96]{0:T(128)S(1)} %reshape.237, f32[96,4,2,25]{3,1,2,0:T(4,128)S(1)} %copy.112), kind=kCustom, calls=%fused_computation.5 | custom fusion | flops 19200 | bytes 230784 | tf_op jit(solution)/shard_map/scatter-add | solution.py:62
  117.2 1.3 collective-permute-start.4
  118.5 1.3 collective-permute-start.5
  119.8 4.5 %collective-permute-start.6 = (f32[8,4,2,25]{3,1,2,0:T(4,128)S(1)}, f32[8,4,2,25]{3,1,2,0:T(4,128)S(1)}, u32[]{:S(2)}, u32[]{:S(2)}) collective-permute-start(f32[8,4,2,25]{3,1,2,0:T(4,128)S(1)} %get-tuple-element.18), channel_id=1, source_target_pairs={{0,2},{2,4},{4,6},{6,8},{8,10},{10,12},{12,14},{1,3},{3,5},{5,7},{... | collective-permute-start | bytes 19208 | tf_op jit(solution)/shard_map/ppermute | solution.py:15
  124.3 4.6 %collective-permute-start.7 = (f32[8,4,2,25]{3,1,2,0:T(4,128)S(1)}, f32[8,4,2,25]{3,1,2,0:T(4,128)S(1)}, u32[]{:S(2)}, u32[]{:S(2)}) collective-permute-start(f32[8,4,2,25]{3,1,2,0:T(4,128)S(1)} %get-tuple-element.17), channel_id=1, source_target_pairs={{0,4},{2,6},{4,8},{6,10},{8,12},{10,14},{1,5},{3,7},{5,9},{7,11},{... | collective-permute-start | bytes 19208 | tf_op jit(solution)/shard_map/ppermute | solution.py:15
  129.1 1.4 collective-permute-done.7
  130.5 1.8 %scatter_fusion.1 = f32[49,4,2,25]{3,1,2,0:T(4,128)S(1)} fusion(f32[49,4,2,25]{3,1,2,0:T(4,128)S(1)} %broadcast_in_dim.28, s32[32]{0:T(128)S(1)} %fusion.54, f32[32,4,2,25]{3,1,2,0:T(4,128)S(1)} %pad_maximum_fusion), kind=kCustom, calls=%fused_computation.6 | custom fusion | flops 6400 | bytes 76928 | tf_op jit(solution)/shard_map/scatter-add | solution.py:67
  133.4 18.5 %psum.7 = f32[4,2]{0,1:T(2,128)S(1)} all-reduce(f32[4,2]{0,1:T(2,128)S(1)} %pad_maximum_fusion.3), channel_id=1, replica_groups=mesh['groups'=2,'sub'=4,'coarse'=2,'rep'=2] {'sub','coarse'}, use_global_device_ids=true, to_apply=%region_4.5 | all-reduce | flops 8 | bytes 64 | tf_op jit(solution)/shard_map/psum | solution.py:98
  (90 shorter events, 18.5 us)
Async XLA Ops:
  0.6 68.1 %copy-start.1 = (bf16[2,64,1200]{2,1,0:T(8,128)(2,1)S(1)}, bf16[2,64,1200]{2,1,0:T(8,128)(2,1)}, u32[]{:S(2)}) copy-start(bf16[2,64,1200]{2,1,0:T(8,128)(2,1)} %param.10) | copy-start | bytes 921604
  0.6 62.2 %copy-start.3 = (bf16[2,32,512]{2,1,0:T(8,128)(2,1)S(1)}, bf16[2,32,512]{2,1,0:T(8,128)(2,1)}, u32[]{:S(2)}) copy-start(bf16[2,32,512]{2,1,0:T(8,128)(2,1)} %param.11) | copy-start | bytes 196612
  0.7 69.5 %copy-start = (bf16[1,720000]{1,0:T(2,128)(2,1)S(1)}, bf16[1,720000]{1,0:T(2,128)(2,1)}, u32[]{:S(2)}) copy-start(bf16[1,720000]{1,0:T(2,128)(2,1)} %param.7) | copy-start | bytes 4320004
  5.0 101.4 %collective-permute-start = (bf16[4,2,8,25]{3,0,1,2:T(4,128)(2,1)}, bf16[4,2,8,25]{3,0,1,2:T(4,128)(2,1)}, u32[]{:S(2)}, u32[]{:S(2)}) collective-permute-start(bf16[4,2,8,25]{3,0,1,2:T(4,128)(2,1)} %bitcast.3), channel_id=1, source_target_pairs={{0,4},{2,6},{4,8},{6,10},{8,12},{10,14},{1,5},{3,7},{5,9},{7,11},{... | collective-permute-start | bytes 9608 | tf_op jit(solution)/shard_map/ppermute | solution.py:15
  11.7 95.5 %collective-permute-start.1 = (bf16[4,2,8,25]{3,0,1,2:T(4,128)(2,1)}, bf16[4,2,8,25]{3,0,1,2:T(4,128)(2,1)}, u32[]{:S(2)}, u32[]{:S(2)}) collective-permute-start(bf16[4,2,8,25]{3,0,1,2:T(4,128)(2,1)} %bitcast.6), channel_id=1, source_target_pairs={{0,2},{2,4},{4,6},{6,8},{8,10},{10,12},{12,14},{1,3},{3,5},{5,7},{... | collective-permute-start | bytes 9608 | tf_op jit(solution)/shard_map/ppermute | solution.py:15
  16.9 91.1 %collective-permute-start.2 = (bf16[4,2,8,25]{3,0,1,2:T(4,128)(2,1)}, bf16[4,2,8,25]{3,0,1,2:T(4,128)(2,1)}, u32[]{:S(2)}, u32[]{:S(2)}) collective-permute-start(bf16[4,2,8,25]{3,0,1,2:T(4,128)(2,1)} %bitcast.9), channel_id=1, source_target_pairs={{2,0},{4,2},{6,4},{8,6},{10,8},{12,10},{14,12},{3,1},{5,3},{7,5},{... | collective-permute-start | bytes 9608 | tf_op jit(solution)/shard_map/ppermute | solution.py:15
  19.3 89.4 %collective-permute-start.3 = (bf16[4,2,8,25]{3,0,1,2:T(4,128)(2,1)}, bf16[4,2,8,25]{3,0,1,2:T(4,128)(2,1)}, u32[]{:S(2)}, u32[]{:S(2)}) collective-permute-start(bf16[4,2,8,25]{3,0,1,2:T(4,128)(2,1)} %bitcast.12), channel_id=1, source_target_pairs={{4,0},{6,2},{8,4},{10,6},{12,8},{14,10},{5,1},{7,3},{9,5},{11,7},{... | collective-permute-start | bytes 9608 | tf_op jit(solution)/shard_map/ppermute | solution.py:15
  64.1 4.4 %all-to-all-start = ((bf16[2,2,128]{2,1,0:T(2,128)(2,1)}), bf16[2,2,128]{2,1,0:T(2,128)(2,1)S(1)}, u32[]{:S(2)}, u32[]{:S(2)}) async-start(bf16[2,2,128]{2,1,0:T(2,128)(2,1)} %reshape.255), calls=%async_computation | async-start | bytes 2048 | tf_op jit(solution)/shard_map/all_to_all | solution.py:90
  101.2 5.3 %copy-start.2 = (bf16[4,2,81,25]{3,0,2,1:T(4,128)(2,1)S(1)}, bf16[4,2,81,25]{3,0,2,1:T(4,128)(2,1)}, u32[]{:S(2)}) copy-start(bf16[4,2,81,25]{3,0,2,1:T(4,128)(2,1)} %get-tuple-element.23) | copy-start | bytes 97204
  112.7 19.9 %copy-start.4 = (f32[4,2,1200]{2,0,1:T(4,128)S(1)}, f32[4,2,1200]{2,0,1:T(4,128)}, u32[]{:S(2)}) copy-start(f32[4,2,1200]{2,0,1:T(4,128)} %get-tuple-element.14) | copy-start | bytes 115204
  117.2 11.9 %collective-permute-start.4 = (f32[8,4,2,25]{3,1,2,0:T(4,128)S(1)}, f32[8,4,2,25]{3,1,2,0:T(4,128)S(1)}, u32[]{:S(2)}, u32[]{:S(2)}) collective-permute-start(f32[8,4,2,25]{3,1,2,0:T(4,128)S(1)} %get-tuple-element.16), channel_id=1, source_target_pairs={{4,0},{6,2},{8,4},{10,6},{12,8},{14,10},{5,1},{7,3},{9,5},{11,7},{... | collective-permute-start | bytes 19208 | tf_op jit(solution)/shard_map/ppermute | solution.py:15
  118.5 10.6 %collective-permute-start.5 = (f32[8,4,2,25]{3,1,2,0:T(4,128)S(1)}, f32[8,4,2,25]{3,1,2,0:T(4,128)S(1)}, u32[]{:S(2)}, u32[]{:S(2)}) collective-permute-start(f32[8,4,2,25]{3,1,2,0:T(4,128)S(1)} %get-tuple-element.19), channel_id=1, source_target_pairs={{2,0},{4,2},{6,4},{8,6},{10,8},{12,10},{14,12},{3,1},{5,3},{7,5},{... | collective-permute-start | bytes 19208 | tf_op jit(solution)/shard_map/ppermute | solution.py:15
  119.8 9.3 %collective-permute-start.6 = (f32[8,4,2,25]{3,1,2,0:T(4,128)S(1)}, f32[8,4,2,25]{3,1,2,0:T(4,128)S(1)}, u32[]{:S(2)}, u32[]{:S(2)}) collective-permute-start(f32[8,4,2,25]{3,1,2,0:T(4,128)S(1)} %get-tuple-element.18), channel_id=1, source_target_pairs={{0,2},{2,4},{4,6},{6,8},{8,10},{10,12},{12,14},{1,3},{3,5},{5,7},{... | collective-permute-start | bytes 19208 | tf_op jit(solution)/shard_map/ppermute | solution.py:15
  124.3 6.1 %collective-permute-start.7 = (f32[8,4,2,25]{3,1,2,0:T(4,128)S(1)}, f32[8,4,2,25]{3,1,2,0:T(4,128)S(1)}, u32[]{:S(2)}, u32[]{:S(2)}) collective-permute-start(f32[8,4,2,25]{3,1,2,0:T(4,128)S(1)} %get-tuple-element.17), channel_id=1, source_target_pairs={{0,4},{2,6},{4,8},{6,10},{8,12},{10,14},{1,5},{3,7},{5,9},{7,11},{... | collective-permute-start | bytes 19208 | tf_op jit(solution)/shard_map/ppermute | solution.py:15
where the time goes:
time: 153 us; the launch traced here: 152 us
  blocking collectives  54.1 us (35%)
  other arithmetic  40.8 us (27%)
  starting transfers between devices  26.9 us (18%)
  local copies, waits for them, and re-layouts  20.7 us (14%)
  matrix products  7.04 us (5%)
  waiting for transfers between devices  1.9 us (1%)
    all_gather x1, blocking collectives, on_device(): piece = lax.all_gather(everyone, ('sub', 'coarse'), axis=1, tiled=True)  33.8 us
    unnamed x1, other arithmetic  31 us
    ppermute x8, starting transfers between devices, passed_along(): return lax.ppermute(array, axis, pairs)  23.7 us
    psum x1, blocking collectives, on_device(): lax.psum(jnp.stack([part_re, part_im], 1), ('sub', 'coarse')) / total  18.5 us
    unnamed x19, local copies, waits for them, and re-layouts  5.48 us
    reshape x1, local copies, waits for them, and re-layouts, on_device(): operators = elem_inv.reshape(nelem, 2, edof, edof)  5.25 us
    gather x4, local copies, waits for them, and re-layouts, on_device(): packed = padded[:, :, outgoing[slot]]  4.69 us
    dot_general x4, matrix products, contract_last(): lax.dot_general(left, right, (((1,), (1,)), ((), ())), preferred_element_...  4.28 us
  transfers between devices with their start and end apart: 9, of which 2 were waited for; matrix products, arithmetic and copies ran while one was open for 34% of the time, Pallas kernels for 0%

commit v1 on v0

v1 whole, which is shorter than its diff:
```python
import functools

import jax
import jax.numpy as jnp
from jax import lax
from jax.experimental import pallas as pl
from jax.experimental.pallas import tpu as pltpu
from jax.sharding import PartitionSpec as P

FACE_DOF = 25
OFFSETS = (-2, -1, 1, 2)
BF = jnp.bfloat16
F32 = jnp.float32
MESH = pl.DeviceIdType.MESH


def iota(shape, dim):
    return lax.broadcasted_iota(jnp.int32, shape, dim)


def over_25(index):
    return jnp.floor((index.astype(F32) + 0.5) * (1.0 / FACE_DOF)).astype(jnp.int32)


def dot_nt(left, right):
    return lax.dot_general(left, right, (((1,), (1,)), ((), ())), preferred_element_type=F32)


def dot_nn(left, right):
    return lax.dot_general(left, right, (((1,), (0,)), ((), ())), preferred_element_type=F32)


def split2(values):
    high = values.astype(BF)
    return high, (values - high.astype(F32)).astype(BF)


def loop(count, body):
    if count <= 16:
        for i in range(count):
            body(i)
    else:
        def step(i, carry):
            body(i)
            return carry
        lax.fori_loop(0, count, step, 0)


def kernel(
    nsub, ncoarse, total,
    res_ref, elem_ref, faces_ref, send_ref, basis_ref, cinv_ref,
    out_ref, inner_ref,
    flat, rows128, mat0, mat1, v6, ext, xs0, xs1, ys0, ys1,
    halo_out, halo_in, rest_out, rest_in, cfull, ret_out, ret_in, inner_out, inner_in,
    elem_sem, halo_send, halo_recv, rest_send, rest_recv, cinv_send, cinv_recv,
    ret_send, ret_recv, inner_send, inner_recv,
):
    nall = nsub * ncoarse
    length = res_ref.shape[2]
    owned = length // FACE_DOF
    slots = 4 * send_ref.shape[2]
    nelem = faces_ref.shape[1]
    ext_rows = owned + slots
    edof = 6 * FACE_DOF
    nslot = 6 * nelem
    rep = lax.axis_index("rep")
    me = lax.axis_index("sub") * ncoarse + lax.axis_index("coarse")

    elem_copy = pltpu.make_async_copy(elem_ref, flat, elem_sem)
    elem_copy.start()

    def where_is(other):
        return {"sub": other // ncoarse, "coarse": lax.rem(other, ncoarse)}

    def peer(i):
        return lax.rem(me + i + 1, nall)

    barrier = pltpu.get_barrier_semaphore()
    loop(nall - 1, lambda i: pl.semaphore_signal(
        barrier, inc=1, device_id=where_is(peer(i)), device_id_type=MESH))
    pl.semaphore_signal(barrier, inc=1, device_id={"rep": 1 - rep}, device_id_type=MESH)

    rb = jnp.concatenate([res_ref[:, 0, :], res_ref[:, 1, :]], 0).astype(BF)
    rf = rb.astype(F32)
    sign = jnp.where(iota((8, 1), 0) < 4, -1.0, 1.0).astype(F32)

    trace = iota((1, length), 1)
    trace_face = over_25(trace)
    trace_dof = trace - FACE_DOF * trace_face
    face_mask = iota((owned, length), 0) == trace_face
    face_bf = jnp.where(face_mask, 1.0, 0.0).astype(BF)
    lane_col = iota((256, 1), 0)
    lane_dof = jnp.where(lane_col < edof, lane_col - FACE_DOF * over_25(lane_col), -1)
    v6[...] = jnp.where(lane_dof == trace_dof, 1.0, 0.0).astype(BF)

    basis = basis_ref[...].reshape(128, length)
    q = dot_nt(rb, basis)
    rest = q + sign * pltpu.roll(pltpu.roll(q, 64, 1), 4, 0)
    rest = jnp.where(iota((8, 128), 1) < 64, rest.astype(BF).astype(F32), 0.0)
    rest = jnp.where(lax.rem(me, 2) == 1, pltpu.roll(rest, 64, 1), rest)
    rest_out[...] = rest
    rest_in[pl.ds(me, 1)] = rest[None]

    id_row = jnp.concatenate(
        [faces_ref[k:k + 1, :] for k in range(6)] + [send_ref[0, j:j + 1, :] for j in range(4)], 1)
    pick_t = jnp.where(iota((128, 128), 0) == id_row, 1.0, 0.0).astype(F32)
    pick = pick_t.T
    send_id = jnp.sum(pick[nslot:] * (iota((slots, 128), 1) + 1).astype(F32), 1, keepdims=True) - 1.0
    pick_b = pick.astype(BF)
    gather = pick_b[:nslot, :ext_rows]
    packer = pick_b[nslot:, :owned]

    left = jnp.concatenate([face_bf * rb[i:i + 1, :] for i in range(8)], 0)
    tiled = dot_nt(left, v6[...])
    packed = []
    for i in range(8):
        part = tiled[i * owned:(i + 1) * owned]
        ext[i, 0:owned, :] = part
        packed.append(dot_nn(packer, part[:, :128].astype(BF)))
    for j in range(4):
        halo_out[j] = jnp.concatenate([part[j * 8:(j + 1) * 8] for part in packed], 0).astype(BF)

    pl.semaphore_wait(barrier, nall)

    def halo_copy(j):
        return pltpu.make_async_remote_copy(
            src_ref=halo_out.at[j], dst_ref=halo_in.at[j], send_sem=halo_send.at[j],
            recv_sem=halo_recv.at[j], device_id=where_is(jnp.clip(me - OFFSETS[j], 0, nall - 1)),
            device_id_type=MESH)

    def ret_copy(j):
        return pltpu.make_async_remote_copy(
            src_ref=ret_out.at[j], dst_ref=ret_in.at[j], send_sem=ret_send.at[j],
            recv_sem=ret_recv.at[j], device_id=where_is(jnp.clip(me + OFFSETS[j], 0, nall - 1)),
            device_id_type=MESH)

    def rest_copy(i, block):
        return pltpu.make_async_remote_copy(
            src_ref=rest_out, dst_ref=rest_in.at[block], send_sem=rest_send.at[i],
            recv_sem=rest_recv.at[block], device_id=where_is(peer(i)), device_id_type=MESH)

    def inner_copy(i, block):
        return pltpu.make_async_remote_copy(
            src_ref=inner_out, dst_ref=inner_in.at[block], send_sem=inner_send.at[i],
            recv_sem=inner_recv.at[block], device_id=where_is(peer(i)), device_id_type=MESH)

    def cinv_copy(half):
        return pltpu.make_async_remote_copy(
            src_ref=cinv_ref, dst_ref=cfull.at[half], send_sem=cinv_send,
            recv_sem=cinv_recv, device_id={"rep": 1 - rep}, device_id_type=MESH)

    def has_reader(j):
        return (me - OFFSETS[j] >= 0) & (me - OFFSETS[j] < nall)

    def has_source(j):
        return (me + OFFSETS[j] >= 0) & (me + OFFSETS[j] < nall)

    for j in range(4):
        @pl.when(has_reader(j))
        def _():
            halo_copy(j).start()

    loop(nall - 1, lambda i: rest_copy(i, me).start())
    cinv_copy(rep).start()
    cfull[pl.ds(rep, 1)] = cinv_ref[...][None]

    elem_copy.wait()
    per = 75 * 128

    def widen(i, carry):
        start = pl.multiple_of(i * per, 128)
        rows128[pl.ds(i * 75, 75), :] = flat[0:1, pl.ds(start, per)].astype(F32).reshape(75, 128)
        return carry

    lax.fori_loop(0, 75, widen, 0, unroll=5)
    lane75 = iota((75, 128), 1)

    def regroup(i, carry):
        first = (150 * i) // 128
        shift = 128 - (150 * i - 128 * first)
        a = pltpu.roll(rows128[pl.ds(first, 75, stride=75), :], shift, 1)
        b = pltpu.roll(rows128[pl.ds(first + 1, 75, stride=75), :], shift, 1)
        c = pltpu.roll(rows128[pl.ds(first + 2, 75, stride=75), :], shift, 1)
        mat0[pl.ds(i, 75, stride=64), :] = jnp.where(lane75 < shift, a, b)
        mat1[pl.ds(i, 75, stride=64), :] = jnp.where(
            lane75 < edof - 128, jnp.where(lane75 < shift, b, c), 0.0)
        return carry

    lax.fori_loop(0, 64, regroup, 0, unroll=8)

    for j in range(4):
        @pl.when(has_source(j))
        def _():
            halo_copy(j).wait_recv()

        @pl.when(jnp.logical_not(has_source(j)))
        def _():
            halo_in[j] = jnp.zeros((64, 128), BF)

        half0 = halo_in[j].astype(F32)
        half1 = pltpu.roll(half0, 125, 1)
        for i in range(8):
            at = owned + j * 8
            ext[i, at:at + 8, 0:128] = half0[i * 8:(i + 1) * 8]
            ext[i, at:at + 8, 128:256] = half1[i * 8:(i + 1) * 8]

    lane_face = over_25(iota((1, 256), 1))
    slot_col = jnp.concatenate([jnp.full((nelem, 1), k, jnp.int32) for k in range(6)], 0)
    slot_mask = lane_face == slot_col
    for i in range(8):
        taken = jnp.where(slot_mask, dot_nn(gather, ext[i].astype(BF)), 0.0)
        x = taken[:nelem]
        for k in range(1, 6):
            x = x + taken[k * nelem:(k + 1) * nelem]
        xs0[i * nelem:(i + 1) * nelem, :] = x[:, :128]
        xs1[i * nelem:(i + 1) * nelem, :] = x[:, 128:]

    fill = jnp.zeros((8, 256 - edof), F32)
    for e in range(nelem):
        xa = jnp.concatenate(
            [xs0[pl.ds(e, 8, stride=nelem), :], xs1[pl.ds(e, 8, stride=nelem), :]], 1)
        xb = sign * pltpu.roll(xa, 4, 0)
        at = e * 2 * edof
        op_re = jnp.concatenate([mat0[at:at + edof, :], mat1[at:at + edof, :]], 1).astype(BF)
        at = at + edof
        op_im = jnp.concatenate([mat0[at:at + edof, :], mat1[at:at + edof, :]], 1).astype(BF)
        y = dot_nt(xa.astype(BF), op_re) + dot_nt(xb.astype(BF), op_im)
        y = jnp.concatenate([y, fill], 1)
        ys0[pl.ds(e, 8, stride=nelem), :] = y[:, :128]
        ys1[pl.ds(e, 8, stride=nelem), :] = y[:, 128:]

    scatter = pick_t.astype(BF)[:ext_rows, :nslot]
    scatter = jnp.concatenate([scatter, scatter], 1)
    summed = []
    for i in range(8):
        rows = slice(i * nelem, (i + 1) * nelem)
        y = jnp.concatenate([ys0[rows, :], ys1[rows, :]], 1)
        y = jnp.where(slot_mask, jnp.concatenate([y] * 6, 0), 0.0)
        high, low = split2(y)
        summed.append(dot_nn(scatter, jnp.concatenate([high, low], 0)))
    fold_lane = iota((1, 128), 1)
    fold = jnp.where((lane_dof == fold_lane), 1.0, 0.0).astype(BF)
    back = jnp.concatenate(
        [s[owned + j * 8:owned + (j + 1) * 8] for j in range(4) for s in summed], 0)
    high, low = split2(back)
    back = dot_nn(high, fold) + dot_nn(low, fold)
    for j in range(4):
        ret_out[j] = back[j * 64:(j + 1) * 64]

        @pl.when(has_source(j))
        def _():
            ret_copy(j).start()

    def rest_wait(i):
        rest_copy(i, peer(i)).wait_recv()

    loop(nall - 1, rest_wait)
    cinv_copy(1 - rep).wait_recv()
    rest_all = jnp.concatenate(
        [rest_in[2 * p] + rest_in[2 * p + 1] for p in range(nall // 2)], 1).astype(BF)
    w = dot_nt(rest_all, cfull[...].reshape(128, rest_all.shape[1]))
    w = w + sign * pltpu.roll(pltpu.roll(w, 96, 1), 4, 0)
    lane128 = iota((8, 128), 1)
    co = jnp.where(lane128 < 32, w, pltpu.roll(w, 96, 1))[:, :64].astype(BF)
    basis = basis_ref[...]
    coarse = dot_nn(co, basis[0]) + sign * pltpu.roll(dot_nn(co, basis[1]), 4, 0)

    half = 4 * nelem
    x0, x1, y0, y1 = xs0[...], xs1[...], ys0[...], ys1[...]
    part_re = x0 * y0 + x1 * y1
    part_im = x0 * pltpu.roll(y0, half, 0) + x1 * pltpu.roll(y1, half, 0)
    part_re = jnp.sum(part_re.reshape(8, nelem, 128), 1)
    part_im = jnp.sum(part_im.reshape(8, nelem, 128), 1)
    part_re = jnp.sum(part_re, 1, keepdims=True) + jnp.sum(rf * coarse, 1, keepdims=True)
    part_im = jnp.sum(part_im, 1, keepdims=True) + jnp.sum(
        rf * pltpu.roll(coarse, 4, 0), 1, keepdims=True)
    part_im = -sign * part_im
    part_re = jnp.broadcast_to(part_re, (8, 128))
    part_im = jnp.broadcast_to(part_im, (8, 128))
    part_re = part_re + pltpu.roll(part_re, 4, 0)
    part_im = part_im + pltpu.roll(part_im, 4, 0)
    mine = jnp.where(lane128 == 0, part_re, part_im)
    inner_out[...] = mine
    inner_in[pl.ds(me, 1)] = mine[None]
    loop(nall - 1, lambda i: inner_copy(i, me).start())

    result = []
    for i in range(8):
        high, low = split2(summed[i][:owned])
        wide = dot_nn(high, v6[...]) + dot_nn(low, v6[...])
        result.append(jnp.sum(jnp.where(face_mask, wide, 0.0), 0, keepdims=True))
    result = jnp.concatenate(result, 0) + coarse

    for j in range(4):
        @pl.when(has_reader(j))
        def _():
            ret_copy(j).wait_recv()

        @pl.when(jnp.logical_not(has_reader(j)))
        def _():
            ret_in[j] = jnp.zeros((64, 128), F32)

    send_mask = send_id.astype(jnp.int32) == trace_face
    given = []
    for i in range(8):
        got = jnp.concatenate([ret_in[j, i * 8:(i + 1) * 8, :] for j in range(4)], 0)
        high = got.astype(BF).astype(F32)
        got = (high + pltpu.roll(got - high, FACE_DOF, 1)).astype(BF)
        wide = dot_nn(got, v6[0:128, :])
        given.append(jnp.sum(jnp.where(send_mask, wide, 0.0), 0, keepdims=True))
    result = result + jnp.concatenate(given, 0)
    out_ref[:, 0, :] = result[0:4]
    out_ref[:, 1, :] = result[4:8]

    loop(nall - 1, lambda i: inner_copy(i, peer(i)).wait_recv())
    inner_ref[...] = jnp.sum(inner_in[...], 0)[0:4, 0:2] * (1.0 / total)

    for j in range(4):
        @pl.when(has_reader(j))
        def _():
            halo_copy(j).wait_send()

        @pl.when(has_source(j))
        def _():
            ret_copy(j).wait_send()

    cinv_copy(rep).wait_send()

    def sent(i):
        rest_copy(i, me).wait_send()
        inner_copy(i, me).wait_send()

    loop(nall - 1, sent)


def solution(mesh):
    nsub = mesh.shape["sub"]
    ncoarse = mesh.shape["coarse"]
    nall = nsub * ncoarse
    placed = (
        P("rep", None, ("groups", "sub", "coarse")),
        P(("groups", "sub", "coarse"), None),
        P(("groups", "sub", "coarse"), None),
        P(("groups", "sub", "coarse"), None, None),
        P(None, ("groups", "sub", "coarse"), None),
        P(None, ("groups", "sub", "coarse", "rep"), None),
    )

    def on_device(residual, elem_inv, elem_faces, send_faces, coarse_basis, coarse_inv):
        length = residual.shape[2]
        count = elem_inv.shape[1]
        vmem = pl.BlockSpec(memory_space=pltpu.VMEM)
        anywhere = pl.BlockSpec(memory_space=pl.ANY)
        dma = pltpu.SemaphoreType.DMA
        return pl.pallas_call(
            functools.partial(kernel, nsub, ncoarse, length * nall),
            out_shape=(
                jax.ShapeDtypeStruct(residual.shape, F32),
                jax.ShapeDtypeStruct((residual.shape[0], 2), F32),
            ),
            in_specs=[vmem, anywhere, vmem, vmem, vmem, vmem],
            out_specs=(vmem, vmem),
            scratch_shapes=[
                pltpu.VMEM((1, count), BF),
                pltpu.VMEM((count // 128 + 7, 128), F32),
                pltpu.VMEM((count // 150, 128), F32),
                pltpu.VMEM((count // 150, 128), F32),
                pltpu.VMEM((256, length), BF),
                pltpu.VMEM((8, 80, 256), F32),
                pltpu.VMEM((128, 128), F32),
                pltpu.VMEM((128, 128), F32),
                pltpu.VMEM((128, 128), F32),
                pltpu.VMEM((128, 128), F32),
                pltpu.VMEM((4, 64, 128), BF),
                pltpu.VMEM((4, 64, 128), BF),
                pltpu.VMEM((8, 128), F32),
                pltpu.VMEM((nall, 8, 128), F32),
                pltpu.VMEM((2,) + coarse_inv.shape, BF),
                pltpu.VMEM((4, 64, 128), F32),
                pltpu.VMEM((4, 64, 128), F32),
                pltpu.VMEM((8, 128), F32),
                pltpu.VMEM((nall, 8, 128), F32),
                dma, dma((4,)), dma((4,)), dma((nall,)), dma((nall,)), dma, dma,
                dma((4,)), dma((4,)), dma((nall,)), dma((nall,)),
            ],
            compiler_params=pltpu.CompilerParams(
                collective_id=0, has_side_effects=True, vmem_limit_bytes=56 << 20),
        )(residual, elem_inv, elem_faces.T, send_faces, coarse_basis, coarse_inv)

    return jax.shard_map(
        on_device,
        mesh=mesh,
        in_specs=placed,
        out_specs=(P("rep", None, ("groups", "sub", "coarse")), P(("groups", "rep"), None)),
        check_vma=False,
    )
```

time: 153 us -> 24 us (0.16)
  blocking collectives: 54.1 us -> 0 us
  other arithmetic: 40.8 us -> 0 us
  starting transfers between devices: 26.9 us -> 0 us
  Pallas kernels: 0 us -> 20.5 us
  local copies, waits for them, and re-layouts: 20.7 us -> 2.7 us
  matrix products: 7.04 us -> 0 us
  waiting for transfers between devices: 1.9 us -> 0 us
    all_gather x2 -> x0, blocking collectives: 35.6 us -> none  [the longest x1 33.8 us: on_device(): piece = lax.all_gather(everyone, ('sub', 'coarse'), axis=1, tiled=True)]
    unnamed x1 -> x0, other arithmetic: 31 us -> none
    ppermute x8 -> x0, starting transfers between devices: 23.7 us -> none  [passed_along(): return lax.ppermute(array, axis, pairs)]
    pallas_call x0 -> x1, Pallas kernels: none -> 20.5 us  [on_device(): pl.pallas_call(functools.partial(kernel, nsub, ncoarse, length * nall), o...]
    psum x1 -> x0, blocking collectives: 18.5 us -> none  [on_device(): lax.psum(jnp.stack([part_re, part_im], 1), ('sub', 'coarse')) / total]
    dot_general x16 -> x0, matrix products: 7.04 us -> none  [the longest x4 4.28 us: contract_last(): lax.dot_general(left, right, (((1,), (1,)), ((), ())), preferred_element_...]
    reshape x6 -> x0, local copies, waits for them, and re-layouts: 6.43 us -> none  [the longest x1 5.25 us: on_device(): operators = elem_inv.reshape(nelem, 2, edof, edof)]
    scatter-add x2 -> x0, other arithmetic: 5.85 us -> none  [the longest x1 4.06 us: on_device(): jax.ops.segment_sum(jnp.moveaxis(local, 2, 0), lookup, num_segments=dead...]
  transfers between devices with their start and end apart: 9 -> 0, of which waited for: 2 -> 0; matrix products, arithmetic and copies ran while one was open for 34% -> 0% of each run, Pallas kernels for 0% -> 0%
where the time goes in v1:
time: 24 us; the launch traced here: 23.8 us
  Pallas kernels  20.5 us (85%)
  local copies, waits for them, and re-layouts  2.7 us (11%)
  between operations  0.64 us (3%)
    pallas_call x1, Pallas kernels, on_device(): pl.pallas_call(functools.partial(kernel, nsub, ncoarse, length * nall), o...  20.5 us
    unnamed x1, local copies, waits for them, and re-layouts  1.4 us
    pallas_call x1, local copies, waits for them, and re-layouts, on_device(): pl.pallas_call(functools.partial(kernel, nsub, ncoarse, length * nall), o...  1.3 us

profile of v1, /device:TPU:0, one launch (start us, length us, event | category | flops | bytes accessed | tf_op | source)
XLA Modules:
  0.0 23.8 jit_solution(6487087399665098416)
XLA Ops:
  0.6 20.5 %shard_map.77 = (f32[4,2,1200]{2,1,0:T(2,128)}, f32[4,2]{1,0:T(4,128)}) custom-call(f32[4,2,1200]{2,1,0:T(2,128)} %res_ref.1, bf16[1,720000]{1,0:T(2,128)(2,1)} %elem_ref.1, s32[6,16]{1,0:T(8,128)} %bitcast.1, s32[1,4,8]{2,1,0:T(4,128)} %send_ref.1, bf16[2,64,1200]{2,1,0:T(8,128)(2,1)} %basis_ref.1, bf16[2,32,512]{2,1,0:T(8,128)(2,1)} %cinv_ref.1), custom_call_target="tpu_custom_call" | custom-call | tf_op jit(solution)/shard_map/pallas_call | solution.py:355
  21.1 1.3 %copy.8 = f32[4,2]{0,1:T(2,128)} copy(f32[4,2]{1,0:T(4,128)} %get-tuple-element.3) | data formatting | bytes 64 | tf_op jit(solution)/shard_map/pallas_call | solution.py:355
  22.4 1.4 %copy.10 = f32[4,2,1200]{2,1,0:T(2,128)} copy(f32[4,2,1200]{2,1,0:T(2,128)} %get-tuple-element.6) | data formatting | bytes 76800

commit v2 on v1

--- a/solution.py
+++ b/solution.py
@@ -49,7 +49,7 @@
 def kernel(
     nsub, ncoarse, total,
     res_ref, elem_ref, faces_ref, send_ref, basis_ref, cinv_ref,
-    out_ref, inner_ref,
+    out_ref,
     flat, rows128, mat0, mat1, v6, ext, xs0, xs1, ys0, ys1,
     halo_out, halo_in, rest_out, rest_in, cfull, ret_out, ret_in, inner_out, inner_in,
     elem_sem, halo_send, halo_recv, rest_send, rest_recv, cinv_send, cinv_recv,
@@ -165,28 +165,34 @@
     cfull[pl.ds(rep, 1)] = cinv_ref[...][None]
 
     elem_copy.wait()
-    per = 75 * 128
+    count = flat.shape[1]
+    nrows = count // 128
+    full = nrows // 64
 
     def widen(i, carry):
-        start = pl.multiple_of(i * per, 128)
-        rows128[pl.ds(i * 75, 75), :] = flat[0:1, pl.ds(start, per)].astype(F32).reshape(75, 128)
+        start = pl.multiple_of(i * 8192, 8192)
+        to = pl.multiple_of(i * 64, 64)
+        rows128[pl.ds(to, 64), :] = flat[0:1, pl.ds(start, 8192)].astype(F32).reshape(64, 128)
         return carry
 
-    lax.fori_loop(0, 75, widen, 0, unroll=5)
+    lax.fori_loop(0, full, widen, 0, unroll=3)
+    rest_rows = nrows - full * 64
+    rows128[full * 64:nrows, :] = flat[0:1, full * 8192:count].astype(F32).reshape(rest_rows, 128)
     lane75 = iota((75, 128), 1)
-
-    def regroup(i, carry):
-        first = (150 * i) // 128
-        shift = 128 - (150 * i - 128 * first)
-        a = pltpu.roll(rows128[pl.ds(first, 75, stride=75), :], shift, 1)
-        b = pltpu.roll(rows128[pl.ds(first + 1, 75, stride=75), :], shift, 1)
-        c = pltpu.roll(rows128[pl.ds(first + 2, 75, stride=75), :], shift, 1)
-        mat0[pl.ds(i, 75, stride=64), :] = jnp.where(lane75 < shift, a, b)
-        mat1[pl.ds(i, 75, stride=64), :] = jnp.where(
-            lane75 < edof - 128, jnp.where(lane75 < shift, b, c), 0.0)
-        return carry
-
-    lax.fori_loop(0, 64, regroup, 0, unroll=8)
+    for i in range(64):
+        first = (edof * i) // 128
+        skip = edof * i - 128 * first
+        shift = 128 - skip
+
+        def turned(row):
+            block = rows128[pl.ds(row, 75, stride=75), :]
+            return pltpu.roll(block, shift, 1) if skip else block
+
+        a = turned(first)
+        b = turned(first + 1)
+        mat0[pl.ds(i, 75, stride=64), :] = jnp.where(lane75 < shift, a, b) if skip else a
+        mat1[pl.ds(i, 75, stride=64), :] = (
+            jnp.where(lane75 < shift, b, turned(first + 2)) if skip + edof > 256 else b)
 
     for j in range(4):
         @pl.when(has_source(j))
@@ -309,11 +315,9 @@
         wide = dot_nn(got, v6[0:128, :])
         given.append(jnp.sum(jnp.where(send_mask, wide, 0.0), 0, keepdims=True))
     result = result + jnp.concatenate(given, 0)
-    out_ref[:, 0, :] = result[0:4]
-    out_ref[:, 1, :] = result[4:8]
-
+    out_ref[:, 0:length] = result
     loop(nall - 1, lambda i: inner_copy(i, peer(i)).wait_recv())
-    inner_ref[...] = jnp.sum(inner_in[...], 0)[0:4, 0:2] * (1.0 / total)
+    out_ref[:, length:length + 128] = jnp.sum(inner_in[...], 0) * (1.0 / total)
 
     for j in range(4):
         @pl.when(has_reader(j))
@@ -331,6 +335,13 @@
         inner_copy(i, me).wait_send()
 
     loop(nall - 1, sent)
+
+
+def deliver(full_ref, out_ref, inner_ref):
+    length = out_ref.shape[2]
+    out_ref[:, 0, :] = full_ref[0:4, 0:length]
+    out_ref[:, 1, :] = full_ref[4:8, 0:length]
+    inner_ref[...] = full_ref[0:4, length:length + 128].T[0:2]
 
 
 def solution(mesh):
@@ -352,14 +363,11 @@
         vmem = pl.BlockSpec(memory_space=pltpu.VMEM)
         anywhere = pl.BlockSpec(memory_space=pl.ANY)
         dma = pltpu.SemaphoreType.DMA
-        return pl.pallas_call(
+        full = pl.pallas_call(
             functools.partial(kernel, nsub, ncoarse, length * nall),
-            out_shape=(
-                jax.ShapeDtypeStruct(residual.shape, F32),
-                jax.ShapeDtypeStruct((residual.shape[0], 2), F32),
-            ),
+            out_shape=jax.ShapeDtypeStruct((8, length + 128), F32),
             in_specs=[vmem, anywhere, vmem, vmem, vmem, vmem],
-            out_specs=(vmem, vmem),
+            out_specs=vmem,
             scratch_shapes=[
                 pltpu.VMEM((1, count), BF),
                 pltpu.VMEM((count // 128 + 7, 128), F32),
@@ -386,6 +394,16 @@
             compiler_params=pltpu.CompilerParams(
                 collective_id=0, has_side_effects=True, vmem_limit_bytes=56 << 20),
         )(residual, elem_inv, elem_faces.T, send_faces, coarse_basis, coarse_inv)
+        out, inner = pl.pallas_call(
+            deliver,
+            out_shape=(
+                jax.ShapeDtypeStruct(residual.shape, F32),
+                jax.ShapeDtypeStruct((2, residual.shape[0]), F32),
+            ),
+            in_specs=[vmem],
+            out_specs=(vmem, vmem),
+        )(full)
+        return out, inner.T
 
     return jax.shard_map(
         on_device,

time: 24 us -> 22.3 us (0.929)
  local copies, waits for them, and re-layouts: 2.7 us -> 0 us
  Pallas kernels: 20.5 us -> 21.5 us
    pallas_call x0 -> x1, Pallas kernels: none -> 1.49 us  [on_device(): pl.pallas_call(deliver, out_shape=(jax.ShapeDtypeStruct(residual.shape, F...]
    unnamed x1 -> x0, local copies, waits for them, and re-layouts: 1.4 us -> none
    pallas_call x1 -> x0, local copies, waits for them, and re-layouts: 1.3 us -> none  [on_device(): pl.pallas_call(functools.partial(kernel, nsub, ncoarse, length * nall), o...]
    pallas_call x1, Pallas kernels: 20.5 us -> 20 us  [on_device(): pl.pallas_call(functools.partial(kernel, nsub, ncoarse, length * nall), o...]
where the time goes in v2:
time: 22.3 us; the launch traced here: 22.1 us
  Pallas kernels  21.5 us (96%)
  between operations  0.64 us (3%)
    pallas_call x1, Pallas kernels, on_device(): pl.pallas_call(functools.partial(kernel, nsub, ncoarse, length * nall), o...  20 us
    pallas_call x1, Pallas kernels, on_device(): pl.pallas_call(deliver, out_shape=(jax.ShapeDtypeStruct(residual.shape, F...  1.49 us

profile of v2, /device:TPU:0, one launch (start us, length us, event | category | flops | bytes accessed | tf_op | source)
XLA Modules:
  0.0 22.1 jit_solution(13349020786346445599)
XLA Ops:
  0.6 20.0 %shard_map.77.full_ref = f32[8,1328]{1,0:T(8,128)} custom-call(f32[4,2,1200]{2,1,0:T(2,128)} %res_ref.1, bf16[1,720000]{1,0:T(2,128)(2,1)} %elem_ref.1, s32[6,16]{1,0:T(8,128)} %bitcast.2, s32[1,4,8]{2,1,0:T(4,128)} %send_ref.1, bf16[2,64,1200]{2,1,0:T(8,128)(2,1)} %basis_ref.1, bf16[2,32,512]{2,1,0:T(8,128)(2,1)} %cinv_ref.1), custom_call_target="tpu_custom_call" | custom-call | tf_op jit(solution)/shard_map/pallas_call | solution.py:366
  20.6 1.5 %shard_map.78 = (f32[4,2,1200]{2,1,0:T(2,128)}, f32[2,4]{1,0:T(2,128)}) custom-call(f32[8,1328]{1,0:T(8,128)} %shard_map.77.full_ref), custom_call_target="tpu_custom_call" | custom-call | tf_op jit(solution)/shard_map/pallas_call | solution.py:397

commit v3 on v2

--- a/solution.py
+++ b/solution.py
@@ -50,7 +50,7 @@
     nsub, ncoarse, total,
     res_ref, elem_ref, faces_ref, send_ref, basis_ref, cinv_ref,
     out_ref,
-    flat, rows128, mat0, mat1, v6, ext, xs0, xs1, ys0, ys1,
+    flat, rows128, mat0, mat1, ops, v6, ext, xs0, xs1, ys0, ys1,
     halo_out, halo_in, rest_out, rest_in, cfull, ret_out, ret_in, inner_out, inner_in,
     elem_sem, halo_send, halo_recv, rest_send, rest_recv, cinv_send, cinv_recv,
     ret_send, ret_recv, inner_send, inner_recv,
@@ -194,6 +194,12 @@
         mat1[pl.ds(i, 75, stride=64), :] = (
             jnp.where(lane75 < shift, b, turned(first + 2)) if skip + edof > 256 else b)
 
+    mat0[count // edof:, :] = jnp.zeros((16, 128), F32)
+    mat1[count // edof:, :] = jnp.zeros((16, 128), F32)
+    for b in range(2 * nelem):
+        rows = slice(b * edof, b * edof + 160)
+        ops[b] = jnp.concatenate([mat0[rows, :], mat1[rows, :]], 1).astype(BF)
+
     for j in range(4):
         @pl.when(has_source(j))
         def _():
@@ -226,11 +232,8 @@
         xa = jnp.concatenate(
             [xs0[pl.ds(e, 8, stride=nelem), :], xs1[pl.ds(e, 8, stride=nelem), :]], 1)
         xb = sign * pltpu.roll(xa, 4, 0)
-        at = e * 2 * edof
-        op_re = jnp.concatenate([mat0[at:at + edof, :], mat1[at:at + edof, :]], 1).astype(BF)
-        at = at + edof
-        op_im = jnp.concatenate([mat0[at:at + edof, :], mat1[at:at + edof, :]], 1).astype(BF)
-        y = dot_nt(xa.astype(BF), op_re) + dot_nt(xb.astype(BF), op_im)
+        y = dot_nt(xa.astype(BF), ops[2 * e]) + dot_nt(xb.astype(BF), ops[2 * e + 1])
+        y = y[:, :edof]
         y = jnp.concatenate([y, fill], 1)
         ys0[pl.ds(e, 8, stride=nelem), :] = y[:, :128]
         ys1[pl.ds(e, 8, stride=nelem), :] = y[:, 128:]
@@ -290,12 +293,22 @@
     inner_in[pl.ds(me, 1)] = mine[None]
     loop(nall - 1, lambda i: inner_copy(i, me).start())
 
-    result = []
-    for i in range(8):
-        high, low = split2(summed[i][:owned])
-        wide = dot_nn(high, v6[...]) + dot_nn(low, v6[...])
-        result.append(jnp.sum(jnp.where(face_mask, wide, 0.0), 0, keepdims=True))
-    result = jnp.concatenate(result, 0) + coarse
+    def spread(parts, mask, depth):
+        for start in range(0, length, 256):
+            lanes = slice(start, min(start + 256, length))
+            wide = dot_nn(parts[0], v6[0:depth, lanes])
+            for part in parts[1:]:
+                wide = wide + dot_nn(part, v6[0:depth, lanes])
+            rows = mask.shape[0]
+            keep = mask[:, lanes]
+            total = [
+                jnp.sum(jnp.where(keep, wide[i * rows:(i + 1) * rows], 0.0), 0, keepdims=True)
+                for i in range(8)]
+            yield lanes, jnp.concatenate(total, 0)
+
+    own = jnp.concatenate([part[:owned] for part in summed], 0)
+    for lanes, value in spread(split2(own), face_mask, 256):
+        out_ref[:, lanes] = value + coarse[:, lanes]
 
     for j in range(4):
         @pl.when(has_reader(j))
@@ -307,15 +320,12 @@
             ret_in[j] = jnp.zeros((64, 128), F32)
 
     send_mask = send_id.astype(jnp.int32) == trace_face
-    given = []
-    for i in range(8):
-        got = jnp.concatenate([ret_in[j, i * 8:(i + 1) * 8, :] for j in range(4)], 0)
-        high = got.astype(BF).astype(F32)
-        got = (high + pltpu.roll(got - high, FACE_DOF, 1)).astype(BF)
-        wide = dot_nn(got, v6[0:128, :])
-        given.append(jnp.sum(jnp.where(send_mask, wide, 0.0), 0, keepdims=True))
-    result = result + jnp.concatenate(given, 0)
-    out_ref[:, 0:length] = result
+    got = jnp.concatenate(
+        [ret_in[j, i * 8:(i + 1) * 8, :] for i in range(8) for j in range(4)], 0)
+    high = got.astype(BF).astype(F32)
+    got = (high + pltpu.roll(got - high, FACE_DOF, 1)).astype(BF)
+    for lanes, value in spread((got,), send_mask, 128):
+        out_ref[:, lanes] = out_ref[:, lanes] + value
     loop(nall - 1, lambda i: inner_copy(i, peer(i)).wait_recv())
     out_ref[:, length:length + 128] = jnp.sum(inner_in[...], 0) * (1.0 / total)
 
@@ -371,8 +381,9 @@
             scratch_shapes=[
                 pltpu.VMEM((1, count), BF),
                 pltpu.VMEM((count // 128 + 7, 128), F32),
-                pltpu.VMEM((count // 150, 128), F32),
-                pltpu.VMEM((count // 150, 128), F32),
+                pltpu.VMEM((count // 150 + 16, 128), F32),
+                pltpu.VMEM((count // 150 + 16, 128), F32),
+                pltpu.VMEM((2 * elem_faces.shape[0], 160, 256), BF),
                 pltpu.VMEM((256, length), BF),
                 pltpu.VMEM((8, 80, 256), F32),
                 pltpu.VMEM((128, 128), F32),

time: 22.3 us -> 21.9 us (0.982)
  Pallas kernels: 21.5 us -> 21 us
    pallas_call x1, Pallas kernels: 20 us -> 19.5 us  [on_device(): pl.pallas_call(functools.partial(kernel, nsub, ncoarse, length * nall), o...]
where the time goes in v3:
time: 21.9 us; the launch traced here: 21.7 us
  Pallas kernels  21 us (96%)
  between operations  0.64 us (3%)
    pallas_call x1, Pallas kernels, on_device(): pl.pallas_call(functools.partial(kernel, nsub, ncoarse, length * nall), o...  19.5 us
    pallas_call x1, Pallas kernels, on_device(): pl.pallas_call(deliver, out_shape=(jax.ShapeDtypeStruct(residual.shape, F...  1.49 us

profile of v3, /device:TPU:0, one launch (start us, length us, event | category | flops | bytes accessed | tf_op | source)
XLA Modules:
  0.0 21.7 jit_solution(14163942887225553021)
XLA Ops:
  0.6 19.5 %shard_map.77.full_ref = f32[8,1328]{1,0:T(8,128)} custom-call(f32[4,2,1200]{2,1,0:T(2,128)} %res_ref.1, bf16[1,720000]{1,0:T(2,128)(2,1)} %elem_ref.1, s32[6,16]{1,0:T(8,128)} %bitcast.2, s32[1,4,8]{2,1,0:T(4,128)} %send_ref.1, bf16[2,64,1200]{2,1,0:T(8,128)(2,1)} %basis_ref.1, bf16[2,32,512]{2,1,0:T(8,128)(2,1)} %cinv_ref.1), custom_call_target="tpu_custom_call" | custom-call | tf_op jit(solution)/shard_map/pallas_call | solution.py:376
  20.2 1.5 %shard_map.78 = (f32[4,2,1200]{2,1,0:T(2,128)}, f32[2,4]{1,0:T(2,128)}) custom-call(f32[8,1328]{1,0:T(8,128)} %shard_map.77.full_ref), custom_call_target="tpu_custom_call" | custom-call | tf_op jit(solution)/shard_map/pallas_call | solution.py:408

commit v4 on v3

--- a/solution.py
+++ b/solution.py
@@ -48,11 +48,11 @@
 
 def kernel(
     nsub, ncoarse, total,
-    res_ref, elem_ref, faces_ref, send_ref, basis_ref, cinv_ref,
+    res_ref, elem_ref, faces_ref, send_ref, basis_from, cinv_ref,
     out_ref,
-    flat, rows128, mat0, mat1, ops, v6, ext, xs0, xs1, ys0, ys1,
+    basis_ref, flat, rows128, mat0, mat1, ops, v6, ext, xs0, xs1, ys0, ys1,
     halo_out, halo_in, rest_out, rest_in, cfull, ret_out, ret_in, inner_out, inner_in,
-    elem_sem, halo_send, halo_recv, rest_send, rest_recv, cinv_send, cinv_recv,
+    basis_sem, elem_sem, halo_send, halo_recv, rest_send, rest_recv, cinv_send, cinv_recv,
     ret_send, ret_recv, inner_send, inner_recv,
 ):
     nall = nsub * ncoarse
@@ -67,6 +67,8 @@
     me = lax.axis_index("sub") * ncoarse + lax.axis_index("coarse")
 
     elem_copy = pltpu.make_async_copy(elem_ref, flat, elem_sem)
+    basis_copy = pltpu.make_async_copy(basis_from, basis_ref, basis_sem)
+    basis_copy.start()
     elem_copy.start()
 
     def where_is(other):
@@ -93,14 +95,6 @@
     lane_dof = jnp.where(lane_col < edof, lane_col - FACE_DOF * over_25(lane_col), -1)
     v6[...] = jnp.where(lane_dof == trace_dof, 1.0, 0.0).astype(BF)
 
-    basis = basis_ref[...].reshape(128, length)
-    q = dot_nt(rb, basis)
-    rest = q + sign * pltpu.roll(pltpu.roll(q, 64, 1), 4, 0)
-    rest = jnp.where(iota((8, 128), 1) < 64, rest.astype(BF).astype(F32), 0.0)
-    rest = jnp.where(lax.rem(me, 2) == 1, pltpu.roll(rest, 64, 1), rest)
-    rest_out[...] = rest
-    rest_in[pl.ds(me, 1)] = rest[None]
-
     id_row = jnp.concatenate(
         [faces_ref[k:k + 1, :] for k in range(6)] + [send_ref[0, j:j + 1, :] for j in range(4)], 1)
     pick_t = jnp.where(iota((128, 128), 0) == id_row, 1.0, 0.0).astype(F32)
@@ -160,8 +154,17 @@
         def _():
             halo_copy(j).start()
 
+    cinv_copy(rep).start()
+    basis_copy.wait()
+    basis = basis_ref[...].reshape(128, length)
+    q = dot_nt(rb, basis)
+    rest = q + sign * pltpu.roll(pltpu.roll(q, 64, 1), 4, 0)
+    rest = jnp.where(iota((8, 128), 1) < 64, rest.astype(BF).astype(F32), 0.0)
+    rest = jnp.where(lax.rem(me, 2) == 1, pltpu.roll(rest, 64, 1), rest)
+    rest_out[...] = rest
+    rest_in[pl.ds(me, 1)] = rest[None]
+
     loop(nall - 1, lambda i: rest_copy(i, me).start())
-    cinv_copy(rep).start()
     cfull[pl.ds(rep, 1)] = cinv_ref[...][None]
 
     elem_copy.wait()
@@ -376,9 +379,10 @@
         full = pl.pallas_call(
             functools.partial(kernel, nsub, ncoarse, length * nall),
             out_shape=jax.ShapeDtypeStruct((8, length + 128), F32),
-            in_specs=[vmem, anywhere, vmem, vmem, vmem, vmem],
+            in_specs=[vmem, anywhere, vmem, vmem, anywhere, vmem],
             out_specs=vmem,
             scratch_shapes=[
+                pltpu.VMEM(coarse_basis.shape, BF),
                 pltpu.VMEM((1, count), BF),
                 pltpu.VMEM((count // 128 + 7, 128), F32),
                 pltpu.VMEM((count // 150 + 16, 128), F32),
@@ -399,7 +403,7 @@
                 pltpu.VMEM((4, 64, 128), F32),
                 pltpu.VMEM((8, 128), F32),
                 pltpu.VMEM((nall, 8, 128), F32),
-                dma, dma((4,)), dma((4,)), dma((nall,)), dma((nall,)), dma, dma,
+                dma, dma, dma((4,)), dma((4,)), dma((nall,)), dma((nall,)), dma, dma,
                 dma((4,)), dma((4,)), dma((nall,)), dma((nall,)),
             ],
             compiler_params=pltpu.CompilerParams(

time: 21.9 us -> 21.9 us (level)
  no operation moved by 1% of the time
where the time goes in v4:
time: 21.9 us; the launch traced here: 21.7 us
  Pallas kernels  21.1 us (96%)
  between operations  0.64 us (3%)
    pallas_call x1, Pallas kernels, on_device(): pl.pallas_call(functools.partial(kernel, nsub, ncoarse, length * nall), o...  19.6 us
    pallas_call x1, Pallas kernels, on_device(): pl.pallas_call(deliver, out_shape=(jax.ShapeDtypeStruct(residual.shape, F...  1.49 us

profile of v4, /device:TPU:0, one launch (start us, length us, event | category | flops | bytes accessed | tf_op | source)
XLA Modules:
  0.0 21.7 jit_solution(17451925521745677838)
XLA Ops:
  0.6 19.6 %shard_map.77.full_ref = f32[8,1328]{1,0:T(8,128)} custom-call(f32[4,2,1200]{2,1,0:T(2,128)} %res_ref.1, bf16[1,720000]{1,0:T(2,128)(2,1)} %elem_ref.1, s32[6,16]{1,0:T(8,128)} %bitcast.2, s32[1,4,8]{2,1,0:T(4,128)} %send_ref.1, bf16[2,64,1200]{2,1,0:T(8,128)(2,1)} %basis_from.1, bf16[2,32,512]{2,1,0:T(8,128)(2,1)} %cinv_ref.1), custom_call_target="tpu_custom_call" | custom-call | tf_op jit(solution)/shard_map/pallas_call | solution.py:379
  20.2 1.5 %shard_map.78 = (f32[4,2,1200]{2,1,0:T(2,128)}, f32[2,4]{1,0:T(2,128)}) custom-call(f32[8,1328]{1,0:T(8,128)} %shard_map.77.full_ref), custom_call_target="tpu_custom_call" | custom-call | tf_op jit(solution)/shard_map/pallas_call | solution.py:412
